TPU v7x, 128 devices: a whole 4x4x4 slice. The times are simulated.
128 devices in a mesh: row: 8 (over x, z_hi), col: 16 (over y, z_lo, core).
Axes of the slice: x: 4, y: 4, z: 4 (z_hi: 2, z_lo: 2; z = z_hi * 2 + z_lo), core: 2. Of those that a mesh axis runs over, the one named last changes fastest.
Arguments:
- amplitudes: bfloat16 [16384, 512], P(('row', 'col')), may hold values from -6 to 6
- integrals: bfloat16 [512, 65536], P('row', 'col'), may hold values from -1 to 1
- pair_list: int32 [2, 16384], P(None, 'row'), may hold values from 0 to 199
- panel_order: int32 [2], replicated, may hold values from 0 to 1, each once
- occ_energy: float32 [200], replicated, may hold values from -2 to -0.4
- vir_energy: float32 [512], replicated, may hold values from 0.2 to 3
Outputs:
- update: bfloat16 [16384, 65536], P('row', 'col')
Inputs may be any that keep to these rules, and one draw needn't show every extreme that they name: `panel_order`: each of the 2 panel numbers appears once.
All inputs are finite; a program needn't handle non-finite values.
Results may differ from a plain program's by a relative error of at most 0.001.
Values may be sent and summed in bfloat16 or wider, within the bound.
A program may use at most 128 MiB of HBM per device.

v0:
```python
import jax
import jax.numpy as jnp
from jax import lax
from jax.sharding import PartitionSpec as P


def shards(amplitudes, integrals, pair_list, panel_order, occ_energy, vir_energy):
    panel_count = panel_order.shape[0]
    blocked = lax.all_to_all(amplitudes, "col", split_axis=1, concat_axis=0, tiled=True)
    full_ints = lax.all_gather(integrals, "row", axis=0, tiled=True)
    panel_rows = full_ints.shape[0] // panel_count
    blocks = [
        lax.dynamic_slice_in_dim(full_ints, panel_order[which] * panel_rows, panel_rows, 0)
        for which in range(panel_count)
    ]
    window = jnp.concatenate(blocks, 0)
    ladder = jnp.dot(
        lax.all_gather(blocked, "col", axis=1, tiled=True),
        window,
        preferred_element_type=jnp.float32,
    )
    occ_index = jnp.arange(occ_energy.shape[0], dtype=jnp.int32)
    matches = pair_list[:, :, None] == occ_index[None, None, :]
    picked = jnp.sum(jnp.where(matches, occ_energy[None, None, :], jnp.float32(0.0)), axis=2)
    pair_energy = picked[0] + picked[1]
    a_count = ladder.shape[1] // vir_energy.shape[0]
    a_first = lax.axis_index("col") * a_count
    a_energy = lax.dynamic_slice_in_dim(vir_energy, a_first, a_count, 0)
    virt_energy = (a_energy[:, None] + vir_energy[None, :]).reshape(-1)
    return (ladder / (pair_energy[:, None] - virt_energy[None, :])).astype(jnp.bfloat16)


def solution(mesh):
    placed = (P(("row", "col"), None), P("row", "col"), P(None, "row"), P(), P(), P())
    return jax.shard_map(
        shards, mesh=mesh, in_specs=placed, out_specs=P("row", "col"), check_vma=False
    )
```

profile of v0, /device:TPU:0, one launch (start us, length us, event | category | flops | bytes accessed | tf_op | source)
XLA Modules:
  0.0 160.3 jit_solution(4610845410400836851)
XLA Ops:
  6.5 0.0 all-gather.3.cloned.1.call-start
  6.5 0.7 all-gather.3.cloned.1.call-update
  7.3 0.0 all-gather.5.cloned.1.call-start
  7.3 1.0 copy.11
  8.3 12.3 %all_to_all.19 = bf16[128,16,32]{0,2,1:T(8,128)(2,1)S(1)} all-to-all(bf16[128,16,32]{0,2,1:T(8,128)(2,1)S(1)} %bitcast.18), channel_id=1, replica_groups=mesh['row'=8,'col'=16] {'col'}, dimensions={1} | all-to-all | bytes 262144 | tf_op jit(solution)/shard_map/all_to_all | solution.py:9
  20.6 0.6 copy_bitcast_fusion
  21.2 0.0 all-gather.5.cloned.1.call-update
  21.3 1.4 fusion.5
  24.0 0.8 dynamic_slice.11
  24.8 0.8 add_bitcast_fusion
  25.5 1.3 select_reduce_fusion
  26.8 56.9 %all-gather.3.cloned.1.call-done = bf16[512,4096]{1,0:T(8,128)(2,1)} async-done(((bf16[64,4096]{1,0:T(8,128)(2,1)}), bf16[512,4096]{1,0:T(8,128)(2,1)}) %all-gather.3.cloned.1.call-update) | async-done | bytes 4194320 | tf_op jit(solution)/shard_map/all_gather | solution.py:10
  83.8 3.9 %constant_dynamic-slice_fusion.1 = (bf16[256,4096]{1,0:T(8,128)(2,1)S(1)}, bf16[256,4096]{1,0:T(8,128)(2,1)}) fusion(bf16[512,4096]{1,0:T(8,128)(2,1)} %all-gather.3.cloned.1.call-done, s32[]{:T(128)S(6)} %select_n.13, s32[]{:T(128)S(6)} %select_n.14), kind=kLoop, calls=%fused_computation.11 | loop fusion | bytes 8388616 | tf_op jit(solution)/shard_map/dynamic_slice | solution.py:13
  87.7 29.4 %all-gather.5.cloned.1.call-done = bf16[2048,512]{0,1:T(8,128)(2,1)} async-done(((bf16[2048,32]{0,1:T(8,128)(2,1)}), bf16[2048,512]{0,1:T(8,128)(2,1)}) %all-gather.5.cloned.1.call-update) | async-done | bytes 2097168 | tf_op jit(solution)/shard_map/all_gather | solution.py:18
  117.1 15.2 %fusion = bf16[2048,4096]{0,1:T(8,128)(2,1)} fusion(bf16[2048,512]{0,1:T(8,128)(2,1)} %all-gather.5.cloned.1.call-done, f32[4096]{0:T(1024)S(1)} %bitcast.19, f32[2048]{0:T(1024)S(1)} %bitcast.20, bf16[256,4096]{1,0:T(8,128)(2,1)} %get-tuple-element.6, bf16[256,4096]{1,0:T(8,128)(2,1)S(1)} %get-tuple-element.5), kind=kOutput, calls=%fused_computation.1 | convolution fusion | flops 8623489024 | bytes 23093248 | tf_op jit(solution)/shard_map/dot_general | solution.py:17
  132.3 21.2 %copy.13 = bf16[2048,4096]{1,0:T(8,128)(2,1)} copy(bf16[2048,4096]{0,1:T(8,128)(2,1)} %fusion) | data formatting | bytes 33554432 | tf_op jit(solution)/shard_map/convert_element_type | solution.py:30
  (2 shorter events, 0.0 us)
Async XLA Ops:
  6.5 77.2 %all-gather.3.cloned.1.call-start = ((), (), s32[]{:S(2)}) async-start(), calls=%async_computation.1 | async-start | bytes 4718592 | tf_op jit(solution)/shard_map/all_gather | solution.py:10
  7.3 109.8 %all-gather.5.cloned.1.call-start = ((), (), s32[]{:S(2)}) async-start(), calls=%async_computation.2 | async-start | bytes 2228224 | tf_op jit(solution)/shard_map/all_gather | solution.py:18
Sparse Core Ops, SparseCore 0:
  9.7 74.0 all-gather.2
  85.5 31.5 all-gather.4
where the time goes:
time: 162 us; the launch traced here: 160 us
  waiting for transfers between devices  87.1 us (54%)
  local copies, waits for them, and re-layouts  28.9 us (18%)
  matrix products  15.2 us (9%)
  between operations  14.8 us (9%)
  blocking collectives  12.3 us (8%)
  other arithmetic  2.05 us (1%)
    all_gather x1, waiting for transfers between devices, shards(): full_ints = lax.all_gather(integrals, 'row', axis=0, tiled=True)  56.9 us
    all_gather x1, waiting for transfers between devices, shards(): lax.all_gather(blocked, 'col', axis=1, tiled=True)  29.4 us
    convert_element_type x1, local copies, waits for them, and re-layouts, shards(): (ladder / (pair_energy[:, None] - virt_energy[None, :])).astype(jnp.bfloa...  21.2 us
    dot_general x1, matrix products, shards(): jnp.dot(lax.all_gather(blocked, 'col', axis=1, tiled=True), window, prefe...  15.2 us
    all_to_all x1, blocking collectives, shards(): lax.all_to_all(amplitudes, 'col', split_axis=1, concat_axis=0, tiled=True)  12.3 us
    dynamic_slice x1, local copies, waits for them, and re-layouts, shards(): lax.dynamic_slice_in_dim(full_ints, panel_order[which] * panel_rows, pane...  3.91 us
  transfers between devices with their start and end apart: 2, of which 2 were waited for; matrix products, arithmetic and copies ran while one was open for 6% of the time, Pallas kernels for 0%

commit v1 on v0

v1 whole, which is shorter than its diff:
```python
import functools

import jax
import jax.numpy as jnp
from jax import lax
from jax.experimental import pallas as pl
from jax.experimental.pallas import tpu as pltpu
from jax.sharding import PartitionSpec as P

MESH = pl.DeviceIdType.MESH
PIECES = 8
NEAR = 5
STRIP = 512
ROWS = 64
PAIRS = 128


def ladder_tile(t_ref, w, pe_ref, ve, out):
    acc = jnp.dot(t_ref[...], w[...], preferred_element_type=jnp.float32)
    for lane in range(0, STRIP, 128):
        gap = pe_ref[...] - ve[:, lane : lane + 128]
        out[:, lane : lane + 128] = (acc[:, lane : lane + 128] / gap).astype(jnp.bfloat16)


def gather_kernel(
    ints, amps, pair_list, order_in, occ_in, vir_in, vir_row_in,
    done, t, far, pe, vir_row,
    near, amp_v, pair_v, order, occ, vir, local_sem, small_sem, w_send, w_recv, t_send, t_recv,
):
    row, col = lax.axis_index("row"), lax.axis_index("col")
    x, zh = row // 2, row % 2
    xr, xl = ((row + 2) % 8, col), ((row + 6) % 8, col)
    zz = (row + 1 - 2 * zh, col)
    yr, yl = (row, (col + 4) % 16), (row, (col + 12) % 16)
    zn = (row, col + 2 - 4 * ((col // 2) % 2))
    sib = (row, col + 1 - 2 * (col % 2))

    small = [
        pltpu.make_async_copy(here, there, small_sem.at[k])
        for k, (here, there) in enumerate((
            (amps, amp_v), (order_in, order), (pair_list, pair_v), (occ_in, occ), (vir_in, vir), (vir_row_in, vir_row),
        ))
    ]
    for copy in small:
        copy.start()

    barrier = pltpu.get_barrier_semaphore()
    for peer in (xr, xl, zz, yr, yl, zn, sib):
        pl.semaphore_signal(barrier, inc=1, device_id=peer, device_id_type=MESH)

    small[0].wait()
    small[1].wait()
    first, second = amp_v[:, 0:256], amp_v[:, 256:512]
    stored0 = jnp.full((PAIRS, 256), order[0], jnp.int32) == 0
    stored1 = jnp.full((PAIRS, 256), order[1], jnp.int32) == 1
    mine = pl.multiple_of(col * PAIRS, PAIRS)
    t[pl.ds(mine, PAIRS), 0:256] = jnp.where(stored0, first, second)
    t[pl.ds(mine, PAIRS), 256:512] = jnp.where(stored1, second, first)
    pl.semaphore_wait(barrier, 7)

    def t_rows(dy, dz, dc=0):
        zl, core = (col // 2) % 2, col % 2
        zl = zl + dz * (1 - 2 * zl)
        core = core + dc * (1 - 2 * core)
        at = ((col // 4 + dy) % 4) * 4 + zl * 2 + core
        return t.at[pl.ds(pl.multiple_of(at * PAIRS, PAIRS), PAIRS)]

    def t_copy(dy, dz, sem, peer):
        return pltpu.make_async_remote_copy(
            src_ref=t_rows(dy, dz), dst_ref=t_rows(dy, dz), send_sem=t_send, recv_sem=t_recv.at[sem],
            device_id=peer, device_id_type=MESH,
        )

    def t_wait(dy, dz, sem):
        t_copy(dy, dz, sem, sib).wait_recv()

    def w_of(p):
        return near.at[p] if p < NEAR else far.at[p - NEAR]

    def w_rows(p, dx, dz, lo=0, size=ROWS):
        at = ((x + dx) % 4) * 2 + zh + dz * (1 - 2 * zh)
        return w_of(p).at[pl.ds(pl.multiple_of(at * ROWS + lo, 32), size)]

    def w_copy(p, dx, dz, sem, peer, lo=0, size=ROWS, own=False):
        dst = w_rows(p, dx, dz, lo, size)
        src = ints.at[:, pl.ds(p * STRIP, STRIP)] if own else dst
        return pltpu.make_async_remote_copy(
            src_ref=src, dst_ref=dst, send_sem=w_send.at[p], recv_sem=w_recv.at[p, sem],
            device_id=peer, device_id_type=MESH,
        )

    def w_wait(p, dx, dz, sem):
        w_copy(p, dx, dz, sem, sib).wait_recv()

    t_copy(0, 0, 0, zn).start()
    t_copy(0, 0, 1, yr).start()
    t_copy(0, 0, 2, yl).start()
    t_copy(0, 0, 7, sib).start()
    near_ids, far_ids = list(range(NEAR)), list(range(NEAR, PIECES))
    for p in (5, 0, 6, 1, 7, 2, 3, 4):
        w_copy(p, 0, 0, 0 if p >= NEAR else 1, xr, own=True).start()
        w_copy(p, 0, 0, 1 if p >= NEAR else 3, xl, own=True).start()
        if p < NEAR:
            w_copy(p, 0, 0, 0, zz, own=True).start()
    for p in far_ids:
        w_copy(p, 0, 0, 3, zz, own=True).start()
    own_in = []
    for p in range(PIECES):
        keep = pltpu.make_async_copy(
            ints.at[:, pl.ds(p * STRIP, STRIP)], w_rows(p, 0, 0), local_sem.at[p]
        )
        keep.start()
        own_in.append(keep)

    for copy in small[2:]:
        copy.wait()
    index = pair_v[...]

    def pick(o, found):
        return jnp.where(index == o, occ[o], found)

    picked = lax.fori_loop(0, occ.shape[0], pick, jnp.zeros(index.shape, jnp.float32), unroll=8)
    pair_row = picked[0:1] + picked[1:2]
    for at in range(0, pair_row.shape[1], 128):
        spread = jnp.broadcast_to(pair_row[:, at : at + 128], (128, 128))
        pe[at : at + 128, :] = spread.T

    def near_cross(p):
        w_wait(p, 0, 1, 0)
        w_copy(p, 0, 1, 3, xr).start()
        w_copy(p, 0, 1, 2, xl).start()

    def near_right(p):
        w_wait(p, 3, 0, 1)
        w_copy(p, 3, 0, 3, xr).start()

    def near_left(p):
        w_wait(p, 1, 1, 2)
        w_copy(p, 1, 1, 3, xl).start()

    def far_spread(p):
        w_wait(p, 3, 0, 0)
        w_copy(p, 3, 0, 2, xr, 0, 32).start()
        w_copy(p, 3, 0, 3, zz).start()
        w_wait(p, 1, 0, 1)
        w_copy(p, 1, 0, 2, xl, 32, 32).start()
        w_copy(p, 1, 0, 3, zz).start()

    def far_last(p):
        w_wait(p, 2, 0, 2)
        w_copy(p, 2, 0, 3, zz).start()

    far_spread(5)
    near_cross(0)
    t_wait(0, 1, 0)
    t_copy(0, 1, 3, yr).start()
    t_copy(0, 1, 4, yl).start()
    t_copy(0, 1, 7, sib).start()
    t_wait(3, 0, 1)
    t_copy(3, 0, 5, yr).start()
    t_copy(3, 0, 7, sib).start()
    t_wait(1, 0, 2)
    t_copy(1, 0, 7, sib).start()
    near_cross(1)
    near_right(0)
    far_spread(6)
    near_cross(2)
    near_right(1)
    t_wait(1, 1, 4)
    t_copy(1, 1, 6, yl).start()
    t_copy(1, 1, 7, sib).start()
    t_wait(3, 1, 3)
    t_copy(3, 1, 7, sib).start()
    far_spread(7)
    near_cross(3)
    near_cross(4)
    near_right(2)
    near_right(3)
    near_right(4)
    t_wait(2, 0, 5)
    t_copy(2, 0, 7, sib).start()
    t_wait(2, 1, 6)
    t_copy(2, 1, 7, sib).start()
    near_left(0)
    far_last(5)
    near_left(1)
    near_left(2)
    far_last(6)
    near_left(3)
    far_last(7)
    near_left(4)

    def wait_bytes(ref, sem):
        pltpu.make_async_copy(ref, ref, sem).wait()

    wait_bytes(t.at[pl.ds(0, 8 * PAIRS)], t_recv.at[7])
    for p in near_ids:
        own_in[p].wait()
        wait_bytes(w_of(p).at[pl.ds(0, 4 * ROWS)], w_recv.at[p, 3])
        ve = vir[col * PIECES + p] + vir_row[...]
        ladder_tile(t, w_of(p), pe, ve, done.at[:, pl.ds(p * STRIP, STRIP)])
    for p in far_ids:
        own_in[p].wait()
        wait_bytes(w_of(p).at[pl.ds(0, 4 * ROWS)], w_recv.at[p, 3])
    for p in range(PIECES):
        wait_bytes(w_of(p).at[pl.ds(0, 7 * ROWS)], w_send.at[p])
    wait_bytes(t.at[pl.ds(0, 15 * PAIRS)], t_send)


def finish_kernel(done, t, far, pe, vir_row, vir_in, out, tail, vir, vir_sem, sem):
    col = lax.axis_index("col")
    width = NEAR * STRIP
    copies = [pltpu.make_async_copy(done, out.at[:, pl.ds(0, width)], sem.at[0])]
    copies[0].start()
    vir_copy = pltpu.make_async_copy(vir_in, vir, vir_sem)
    vir_copy.start()
    vir_copy.wait()
    for k in range(PIECES - NEAR):
        ve = vir[col * PIECES + NEAR + k] + vir_row[...]
        ladder_tile(t, far.at[k], pe, ve, tail.at[k])
        copy = pltpu.make_async_copy(
            tail.at[k], out.at[:, pl.ds(width + k * STRIP, STRIP)], sem.at[k + 1]
        )
        copy.start()
        copies.append(copy)
    for copy in copies:
        copy.wait()


def shards(amplitudes, integrals, pair_list, panel_order, occ_energy, vir_energy):
    vmem, hbm = pl.BlockSpec(memory_space=pltpu.VMEM), pl.BlockSpec(memory_space=pltpu.HBM)
    rows, depth, columns = 16 * PAIRS, 8 * ROWS, PIECES * STRIP
    far_count = PIECES - NEAR
    done, t, far, pe, vir_row = pl.pallas_call(
        gather_kernel,
        out_shape=(
            pltpu.VMEM((rows, NEAR * STRIP), jnp.bfloat16),
            pltpu.VMEM((rows, depth), jnp.bfloat16),
            pltpu.VMEM((far_count, depth, STRIP), jnp.bfloat16),
            pltpu.VMEM((rows, 128), jnp.float32),
            pltpu.VMEM((1, vir_energy.shape[0]), jnp.float32),
        ),
        in_specs=[hbm] * 7,
        out_specs=(vmem,) * 5,
        scratch_shapes=[
            pltpu.VMEM((NEAR, depth, STRIP), jnp.bfloat16),
            pltpu.VMEM((PAIRS, depth), jnp.bfloat16),
            pltpu.VMEM((2, rows), jnp.int32),
            pltpu.SMEM((2,), jnp.int32),
            pltpu.SMEM((200,), jnp.float32),
            pltpu.SMEM((512,), jnp.float32),
            pltpu.SemaphoreType.DMA((PIECES,)),
            pltpu.SemaphoreType.DMA((6,)),
            pltpu.SemaphoreType.DMA((PIECES,)),
            pltpu.SemaphoreType.DMA((PIECES, 4)),
            pltpu.SemaphoreType.DMA,
            pltpu.SemaphoreType.DMA((8,)),
        ],
        cost_estimate=pl.CostEstimate(
            flops=2 * rows * depth * NEAR * STRIP, bytes_accessed=4 << 20, transcendentals=0
        ),
        compiler_params=pltpu.CompilerParams(
            collective_id=0, has_side_effects=True, vmem_limit_bytes=32 << 20
        ),
        name="gather",
    )(*(pltpu.with_memory_space_constraint(given, pltpu.HBM) for given in (
        integrals, amplitudes, pair_list, panel_order, occ_energy, vir_energy, vir_energy.reshape(1, -1),
    )))
    return pl.pallas_call(
        finish_kernel,
        out_shape=jax.ShapeDtypeStruct((rows, columns), jnp.bfloat16),
        in_specs=[vmem] * 5 + [hbm],
        out_specs=hbm,
        scratch_shapes=[
            pltpu.VMEM((far_count, rows, STRIP), jnp.bfloat16),
            pltpu.SMEM((512,), jnp.float32),
            pltpu.SemaphoreType.DMA,
            pltpu.SemaphoreType.DMA((far_count + 1,)),
        ],
        cost_estimate=pl.CostEstimate(
            flops=2 * rows * depth * far_count * STRIP,
            bytes_accessed=2 * rows * columns,
            transcendentals=0,
        ),
        compiler_params=pltpu.CompilerParams(vmem_limit_bytes=32 << 20),
        name="finish",
    )(done, t, far, pe, vir_row, pltpu.with_memory_space_constraint(vir_energy, pltpu.HBM))


def solution(mesh):
    placed = (P(("row", "col"), None), P("row", "col"), P(None, "row"), P(), P(), P())
    return jax.shard_map(
        shards, mesh=mesh, in_specs=placed, out_specs=P("row", "col"), check_vma=False
    )
```

time: 162 us -> 43.8 us (0.27)
  waiting for transfers between devices: 87.1 us -> 0 us
  Pallas kernels: 0 us -> 43.7 us
  local copies, waits for them, and re-layouts: 28.9 us -> 0 us
  matrix products: 15.2 us -> 0 us
  between operations: 14.8 us -> 0.01 us
  blocking collectives: 12.3 us -> 0 us
  other arithmetic: 2.05 us -> 0 us
    all_gather x2 -> x0, waiting for transfers between devices: 86.3 us -> none  [the longest x1 56.9 us: shards(): full_ints = lax.all_gather(integrals, 'row', axis=0, tiled=True)]
    pallas_call x0 -> x2, Pallas kernels: none -> 43.7 us  [the longest x1 37.6 us: shards(): pl.pallas_call(gather_kernel, out_shape=(pltpu.VMEM((rows, NEAR * STRIP),...]
    convert_element_type x1 -> x0, local copies, waits for them, and re-layouts: 21.2 us -> none  [shards(): (ladder / (pair_energy[:, None] - virt_energy[None, :])).astype(jnp.bfloa...]
    dot_general x1 -> x0, matrix products: 15.2 us -> none  [shards(): jnp.dot(lax.all_gather(blocked, 'col', axis=1, tiled=True), window, prefe...]
    all_to_all x1 -> x0, blocking collectives: 12.3 us -> none  [shards(): lax.all_to_all(amplitudes, 'col', split_axis=1, concat_axis=0, tiled=True)]
    dynamic_slice x2 -> x0, local copies, waits for them, and re-layouts: 4.68 us -> none  [the longest x1 3.91 us: shards(): lax.dynamic_slice_in_dim(full_ints, panel_order[which] * panel_rows, pane...]
  transfers between devices with their start and end apart: 2 -> 0, of which waited for: 2 -> 0; matrix products, arithmetic and copies ran while one was open for 6% -> 0% of each run, Pallas kernels for 0% -> 0%
where the time goes in v1:
time: 43.8 us; the launch traced here: 43.7 us
  Pallas kernels  43.7 us (100%)
    pallas_call x1, Pallas kernels, shards(): pl.pallas_call(gather_kernel, out_shape=(pltpu.VMEM((rows, NEAR * STRIP),...  37.6 us
    pallas_call x1, Pallas kernels, shards(): pl.pallas_call(finish_kernel, out_shape=jax.ShapeDtypeStruct((rows, colum...  6.08 us

profile of v1, /device:TPU:0, one launch (start us, length us, event | category | flops | bytes accessed | tf_op | source)
XLA Modules:
  0.0 43.7 jit_solution(10071956845344263770)
XLA Ops:
  0.0 37.6 %gather.1 = (bf16[2048,2560]{1,0:T(8,128)(2,1)S(1)}, bf16[2048,512]{1,0:T(8,128)(2,1)S(1)}, bf16[3,512,512]{2,1,0:T(8,128)(2,1)S(1)}, f32[2048,128]{1,0:T(8,128)S(1)}, f32[1,512]{1,0:T(1,128)S(1)}) custom-call(bf16[64,4096]{1,0:T(8,128)(2,1)} %ints.1, bf16[128,512]{1,0:T(8,128)(2,1)} %amps.1, s32[2,2048]{1,0:T(2,128)} %pair_list.1, s32[2]{0:T(128)} %order_in.1, ...), custom_call_target="tpu_custom_call" | custom-call | flops 5368709120 | bytes 4194304 | tf_op jit(solution)/shard_map/gather/pallas_call | solution.py:234
  37.6 6.1 %finish.1 = bf16[2048,4096]{1,0:T(8,128)(2,1)} custom-call(bf16[2048,2560]{1,0:T(8,128)(2,1)S(1)} %get-tuple-element.10.done, bf16[2048,512]{1,0:T(8,128)(2,1)S(1)} %get-tuple-element.11.t, bf16[3,512,512]{2,1,0:T(8,128)(2,1)S(1)} %get-tuple-element.12.far, f32[2048,128]{1,0:T(8,128)S(1)} %get-tuple-element.13.pe, f32[1,512]{1,0:T(1,128)S(1)} %get-tuple-element.14.vir_row, ...), custom_call_target="tpu_custom_call" | custom-call | flops 3221225472 | bytes 16777216 | tf_op jit(solution)/shard_map/finish/pallas_call | solution.py:269

commit v2 on v1

v2 whole, which is shorter than its diff:
```python
import functools

import jax
import jax.numpy as jnp
from jax import lax
from jax.experimental import pallas as pl
from jax.experimental.pallas import tpu as pltpu
from jax.sharding import PartitionSpec as P

MESH = pl.DeviceIdType.MESH
PIECES = 8
EARLY = 5
FAR = (1, 3, 7)
STRIP = 512
ROWS = 64
PAIRS = 128

STEPS = (
    ("ox", 1), ("oz", 4), ("oz", 2), ("ox", 7), ("ox", 5), ("oz", 0), ("pairs", 0), ("t00", 0), ("oz", 5), ("fl", 1),
    ("ox", 3), ("ox", 0), ("fr", 1), ("nc", 2), ("t30", 0), ("ox", 6), ("fr", 3), ("nr", 0), ("t20", 0), ("t01", 0),
    ("oz", 6), ("fl", 3), ("oz", 1), ("ox", 2), ("t10", 0), ("nc", 0), ("ox", 4), ("ff", 1), ("oz", 3), ("t31", 0),
    ("ff", 3), ("t11", 0), ("fr", 7), ("nc", 4), ("nr", 2), ("nl", 0), ("fl", 7), ("nr", 4), ("nr", 5), ("nc", 5),
    ("t21", 0), ("nl", 2), ("nc", 6), ("oz", 7), ("nr", 6), ("ff", 7), ("mul", 0), ("nl", 4), ("nl", 5), ("mul", 1),
    ("nl", 6), ("mul", 2), ("mul", 3), ("mul", 4),
)


def ladder_tile(t_ref, w, pe_ref, ve, out):
    acc = jnp.dot(t_ref[...], w[...], preferred_element_type=jnp.float32)
    for lane in range(0, STRIP, 128):
        gap = pe_ref[...] - ve[:, lane : lane + 128]
        out[:, lane : lane + 128] = (acc[:, lane : lane + 128] / gap).astype(jnp.bfloat16)


def gather_kernel(
    ints, amps, pair_list, order_in, occ_in, vir_in, vir_row_in,
    done, t, late, pe, vir_row,
    early, amp_v, pair_v, order, occ, vir, local_sem, small_sem, w_send, w_recv, t_send, t_recv,
):
    row, col = lax.axis_index("row"), lax.axis_index("col")
    x, zh = row // 2, row % 2
    xr, xl = ((row + 2) % 8, col), ((row + 6) % 8, col)
    zz = (row + 1 - 2 * zh, col)
    yr, yl = (row, (col + 4) % 16), (row, (col + 12) % 16)
    zn = (row, col + 2 - 4 * ((col // 2) % 2))
    sib = (row, col + 1 - 2 * (col % 2))

    small = [
        pltpu.make_async_copy(here, there, small_sem.at[k])
        for k, (here, there) in enumerate((
            (amps, amp_v), (order_in, order), (pair_list, pair_v), (occ_in, occ), (vir_in, vir), (vir_row_in, vir_row),
        ))
    ]
    for copy in small:
        copy.start()

    barrier = pltpu.get_barrier_semaphore()
    for peer in (xr, xl, zz, yr, yl, zn, sib):
        pl.semaphore_signal(barrier, inc=1, device_id=peer, device_id_type=MESH)

    pl.semaphore_wait(barrier, 7)

    def t_rows(dy, dz, dc=0):
        zl, core = (col // 2) % 2, col % 2
        zl = zl + dz * (1 - 2 * zl)
        core = core + dc * (1 - 2 * core)
        at = ((col // 4 + dy) % 4) * 4 + zl * 2 + core
        return t.at[pl.ds(pl.multiple_of(at * PAIRS, PAIRS), PAIRS)]

    def t_copy(dy, dz, sem, peer):
        return pltpu.make_async_remote_copy(
            src_ref=t_rows(dy, dz), dst_ref=t_rows(dy, dz), send_sem=t_send, recv_sem=t_recv.at[sem],
            device_id=peer, device_id_type=MESH,
        )

    def t_wait(dy, dz, sem):
        t_copy(dy, dz, sem, sib).wait_recv()

    def w_of(p):
        return early.at[p] if p < EARLY else late.at[p - EARLY]

    def w_rows(p, dx, dz, lo=0, size=ROWS):
        at = ((x + dx) % 4) * 2 + zh + dz * (1 - 2 * zh)
        return w_of(p).at[pl.ds(pl.multiple_of(at * ROWS + lo, 32), size)]

    def w_copy(p, dx, dz, sem, peer, lo=0, size=ROWS, own=False):
        dst = w_rows(p, dx, dz, lo, size)
        src = ints.at[:, pl.ds(p * STRIP, STRIP)] if own else dst
        return pltpu.make_async_remote_copy(
            src_ref=src, dst_ref=dst, send_sem=w_send.at[p], recv_sem=w_recv.at[p, sem],
            device_id=peer, device_id_type=MESH,
        )

    def w_wait(p, dx, dz, sem):
        w_copy(p, dx, dz, sem, sib).wait_recv()

    own_in = []
    for p in range(PIECES):
        own_in.append(
            pltpu.make_async_copy(ints.at[:, pl.ds(p * STRIP, STRIP)], w_rows(p, 0, 0), local_sem.at[p])
        )

    def ox(p):
        w_copy(p, 0, 0, 0 if p in FAR else 1, xr, own=True).start()
        w_copy(p, 0, 0, 1 if p in FAR else 3, xl, own=True).start()

    def oz(p):
        w_copy(p, 0, 0, 3 if p in FAR else 0, zz, own=True).start()
        own_in[p].start()

    def nc(p):
        w_wait(p, 0, 1, 0)
        w_copy(p, 0, 1, 3, xr).start()
        w_copy(p, 0, 1, 2, xl).start()

    def nr(p):
        w_wait(p, 3, 0, 1)
        w_copy(p, 3, 0, 3, xr).start()

    def nl(p):
        w_wait(p, 1, 1, 2)
        w_copy(p, 1, 1, 3, xl).start()

    def fr(p):
        w_wait(p, 3, 0, 0)
        w_copy(p, 3, 0, 2, xr, 0, 32).start()
        w_copy(p, 3, 0, 3, zz).start()

    def fl(p):
        w_wait(p, 1, 0, 1)
        w_copy(p, 1, 0, 2, xl, 32, 32).start()
        w_copy(p, 1, 0, 3, zz).start()

    def ff(p):
        w_wait(p, 2, 0, 2)
        w_copy(p, 2, 0, 3, zz).start()

    def t00(_):
        small[0].wait()
        small[1].wait()
        first, second = amp_v[:, 0:256], amp_v[:, 256:512]
        stored0 = jnp.full((PAIRS, 256), order[0], jnp.int32) == 0
        stored1 = jnp.full((PAIRS, 256), order[1], jnp.int32) == 1
        mine = pl.multiple_of(col * PAIRS, PAIRS)
        t[pl.ds(mine, PAIRS), 0:256] = jnp.where(stored0, first, second)
        t[pl.ds(mine, PAIRS), 256:512] = jnp.where(stored1, second, first)
        t_copy(0, 0, 0, zn).start()
        t_copy(0, 0, 1, yr).start()
        t_copy(0, 0, 2, yl).start()
        t_copy(0, 0, 7, sib).start()

    def t01(_):
        t_wait(0, 1, 0)
        t_copy(0, 1, 3, yr).start()
        t_copy(0, 1, 4, yl).start()
        t_copy(0, 1, 7, sib).start()

    def t30(_):
        t_wait(3, 0, 1)
        t_copy(3, 0, 5, yr).start()
        t_copy(3, 0, 7, sib).start()

    def t10(_):
        t_wait(1, 0, 2)
        t_copy(1, 0, 7, sib).start()

    def t31(_):
        t_wait(3, 1, 3)
        t_copy(3, 1, 7, sib).start()

    def t11(_):
        t_wait(1, 1, 4)
        t_copy(1, 1, 6, yl).start()
        t_copy(1, 1, 7, sib).start()

    def t20(_):
        t_wait(2, 0, 5)
        t_copy(2, 0, 7, sib).start()

    def t21(_):
        t_wait(2, 1, 6)
        t_copy(2, 1, 7, sib).start()

    def pairs(_):
        for copy in small[2:]:
            copy.wait()
        index = pair_v[...]

        def pick(o, found):
            return jnp.where(index == o, occ[o], found)

        picked = lax.fori_loop(0, occ.shape[0], pick, jnp.zeros(index.shape, jnp.float32), unroll=8)
        pair_row = picked[0:1] + picked[1:2]
        for at in range(0, pair_row.shape[1], 128):
            spread = jnp.broadcast_to(pair_row[:, at : at + 128], (128, 128))
            pe[at : at + 128, :] = spread.T

    def wait_bytes(ref, sem):
        pltpu.make_async_copy(ref, ref, sem).wait()

    def whole(p):
        own_in[p].wait()
        wait_bytes(w_of(p).at[pl.ds(0, 4 * ROWS)], w_recv.at[p, 3])

    def mul(p):
        if p == 0:
            wait_bytes(t.at[pl.ds(0, 8 * PAIRS)], t_recv.at[7])
        whole(p)
        ve = vir[col * PIECES + p] + vir_row[...]
        ladder_tile(t, w_of(p), pe, ve, done.at[:, pl.ds(p * STRIP, STRIP)])

    steps = dict(
        ox=ox, oz=oz, nc=nc, nr=nr, nl=nl, fr=fr, fl=fl, ff=ff, mul=mul, pairs=pairs,
        t00=t00, t01=t01, t30=t30, t10=t10, t31=t31, t11=t11, t20=t20, t21=t21,
    )
    for name, p in STEPS:
        steps[name](p)
    for p in range(EARLY, PIECES):
        whole(p)
    for p in range(PIECES):
        wait_bytes(w_of(p).at[pl.ds(0, 7 * ROWS)], w_send.at[p])
    wait_bytes(t.at[pl.ds(0, 15 * PAIRS)], t_send)


def finish_kernel(done, t, late, pe, vir_row, vir_in, out, tail, vir, vir_sem, sem):
    col = lax.axis_index("col")
    width = EARLY * STRIP
    copies = [pltpu.make_async_copy(done, out.at[:, pl.ds(0, width)], sem.at[0])]
    copies[0].start()
    vir_copy = pltpu.make_async_copy(vir_in, vir, vir_sem)
    vir_copy.start()
    vir_copy.wait()
    for k in range(PIECES - EARLY):
        ve = vir[col * PIECES + EARLY + k] + vir_row[...]
        ladder_tile(t, late.at[k], pe, ve, tail.at[k])
        copy = pltpu.make_async_copy(
            tail.at[k], out.at[:, pl.ds(width + k * STRIP, STRIP)], sem.at[k + 1]
        )
        copy.start()
        copies.append(copy)
    for copy in copies:
        copy.wait()


def shards(amplitudes, integrals, pair_list, panel_order, occ_energy, vir_energy):
    vmem, hbm = pl.BlockSpec(memory_space=pltpu.VMEM), pl.BlockSpec(memory_space=pltpu.HBM)
    rows, depth, columns = 16 * PAIRS, 8 * ROWS, PIECES * STRIP
    late_count = PIECES - EARLY
    done, t, late, pe, vir_row = pl.pallas_call(
        gather_kernel,
        out_shape=(
            pltpu.VMEM((rows, EARLY * STRIP), jnp.bfloat16),
            pltpu.VMEM((rows, depth), jnp.bfloat16),
            pltpu.VMEM((late_count, depth, STRIP), jnp.bfloat16),
            pltpu.VMEM((rows, 128), jnp.float32),
            pltpu.VMEM((1, vir_energy.shape[0]), jnp.float32),
        ),
        in_specs=[hbm] * 7,
        out_specs=(vmem,) * 5,
        scratch_shapes=[
            pltpu.VMEM((EARLY, depth, STRIP), jnp.bfloat16),
            pltpu.VMEM((PAIRS, depth), jnp.bfloat16),
            pltpu.VMEM((2, rows), jnp.int32),
            pltpu.SMEM((2,), jnp.int32),
            pltpu.SMEM((200,), jnp.float32),
            pltpu.SMEM((512,), jnp.float32),
            pltpu.SemaphoreType.DMA((PIECES,)),
            pltpu.SemaphoreType.DMA((6,)),
            pltpu.SemaphoreType.DMA((PIECES,)),
            pltpu.SemaphoreType.DMA((PIECES, 4)),
            pltpu.SemaphoreType.DMA,
            pltpu.SemaphoreType.DMA((8,)),
        ],
        cost_estimate=pl.CostEstimate(
            flops=2 * rows * depth * EARLY * STRIP, bytes_accessed=4 << 20, transcendentals=0
        ),
        compiler_params=pltpu.CompilerParams(
            collective_id=0, has_side_effects=True, vmem_limit_bytes=32 << 20
        ),
        name="gather",
    )(*(pltpu.with_memory_space_constraint(given, pltpu.HBM) for given in (
        integrals, amplitudes, pair_list, panel_order, occ_energy, vir_energy, vir_energy.reshape(1, -1),
    )))
    return pl.pallas_call(
        finish_kernel,
        out_shape=jax.ShapeDtypeStruct((rows, columns), jnp.bfloat16),
        in_specs=[vmem] * 5 + [hbm],
        out_specs=hbm,
        scratch_shapes=[
            pltpu.VMEM((late_count, rows, STRIP), jnp.bfloat16),
            pltpu.SMEM((512,), jnp.float32),
            pltpu.SemaphoreType.DMA,
            pltpu.SemaphoreType.DMA((late_count + 1,)),
        ],
        cost_estimate=pl.CostEstimate(
            flops=2 * rows * depth * late_count * STRIP,
            bytes_accessed=2 * rows * columns,
            transcendentals=0,
        ),
        compiler_params=pltpu.CompilerParams(vmem_limit_bytes=32 << 20),
        name="finish",
    )(done, t, late, pe, vir_row, pltpu.with_memory_space_constraint(vir_energy, pltpu.HBM))


def solution(mesh):
    placed = (P(("row", "col"), None), P("row", "col"), P(None, "row"), P(), P(), P())
    return jax.shard_map(
        shards, mesh=mesh, in_specs=placed, out_specs=P("row", "col"), check_vma=False
    )
```

time: 43.8 us -> 41.7 us (0.952)
  Pallas kernels: 43.7 us -> 41.4 us
    pallas_call x1, Pallas kernels: 37.6 us -> 35.3 us  [shards(): pl.pallas_call(gather_kernel, out_shape=(pltpu.VMEM((rows, EARLY * STRIP)...]
where the time goes in v2:
time: 41.7 us; the launch traced here: 41.4 us
  Pallas kernels  41.4 us (99%)
    pallas_call x1, Pallas kernels, shards(): pl.pallas_call(gather_kernel, out_shape=(pltpu.VMEM((rows, EARLY * STRIP)...  35.3 us
    pallas_call x1, Pallas kernels, shards(): pl.pallas_call(finish_kernel, out_shape=jax.ShapeDtypeStruct((rows, colum...  6.08 us

profile of v2, /device:TPU:0, one launch (start us, length us, event | category | flops | bytes accessed | tf_op | source)
XLA Modules:
  0.0 41.4 jit_solution(4414400736746018063)
XLA Ops:
  0.0 35.3 %gather.1 = (bf16[2048,2560]{1,0:T(8,128)(2,1)S(1)}, bf16[2048,512]{1,0:T(8,128)(2,1)S(1)}, bf16[3,512,512]{2,1,0:T(8,128)(2,1)S(1)}, f32[2048,128]{1,0:T(8,128)S(1)}, f32[1,512]{1,0:T(1,128)S(1)}) custom-call(bf16[64,4096]{1,0:T(8,128)(2,1)} %ints.1, bf16[128,512]{1,0:T(8,128)(2,1)} %amps.1, s32[2,2048]{1,0:T(2,128)} %pair_list.1, s32[2]{0:T(128)} %order_in.1, ...), custom_call_target="tpu_custom_call" | custom-call | flops 5368709120 | bytes 4194304 | tf_op jit(solution)/shard_map/gather/pallas_call | solution.py:249
  35.3 6.1 %finish.1 = bf16[2048,4096]{1,0:T(8,128)(2,1)} custom-call(bf16[2048,2560]{1,0:T(8,128)(2,1)S(1)} %get-tuple-element.10.done, bf16[2048,512]{1,0:T(8,128)(2,1)S(1)} %get-tuple-element.11.t, bf16[3,512,512]{2,1,0:T(8,128)(2,1)S(1)} %get-tuple-element.12.late, f32[2048,128]{1,0:T(8,128)S(1)} %get-tuple-element.13.pe, f32[1,512]{1,0:T(1,128)S(1)} %get-tuple-element.14.vir_row, ...), custom_call_target="tpu_custom_call" | custom-call | flops 3221225472 | bytes 16777216 | tf_op jit(solution)/shard_map/finish/pallas_call | solution.py:284

commit v3 on v2

--- a/solution.py
+++ b/solution.py
@@ -34,8 +34,8 @@
 
 def gather_kernel(
     ints, amps, pair_list, order_in, occ_in, vir_in, vir_row_in,
-    done, t, late, pe, vir_row,
-    early, amp_v, pair_v, order, occ, vir, local_sem, small_sem, w_send, w_recv, t_send, t_recv,
+    done, t, late, pe, late_ve,
+    early, amp_v, pair_v, vir_row, order, occ, vir, local_sem, small_sem, w_send, w_recv, t_send, t_recv,
 ):
     row, col = lax.axis_index("row"), lax.axis_index("col")
     x, zh = row // 2, row % 2
@@ -45,6 +45,10 @@
     zn = (row, col + 2 - 4 * ((col // 2) % 2))
     sib = (row, col + 1 - 2 * (col % 2))
 
+    barrier = pltpu.get_barrier_semaphore()
+    for peer in (xr, xl, zz, yr, yl, zn, sib):
+        pl.semaphore_signal(barrier, inc=1, device_id=peer, device_id_type=MESH)
+
     small = [
         pltpu.make_async_copy(here, there, small_sem.at[k])
         for k, (here, there) in enumerate((
@@ -53,10 +57,6 @@
     ]
     for copy in small:
         copy.start()
-
-    barrier = pltpu.get_barrier_semaphore()
-    for peer in (xr, xl, zz, yr, yl, zn, sib):
-        pl.semaphore_signal(barrier, inc=1, device_id=peer, device_id_type=MESH)
 
     pl.semaphore_wait(barrier, 7)
 
@@ -194,6 +194,8 @@
         for at in range(0, pair_row.shape[1], 128):
             spread = jnp.broadcast_to(pair_row[:, at : at + 128], (128, 128))
             pe[at : at + 128, :] = spread.T
+        for p in range(EARLY, PIECES):
+            late_ve[:, (p - EARLY) * STRIP : (p - EARLY + 1) * STRIP] = vir[col * PIECES + p] + vir_row[...]
 
     def wait_bytes(ref, sem):
         pltpu.make_async_copy(ref, ref, sem).wait()
@@ -215,24 +217,19 @@
     )
     for name, p in STEPS:
         steps[name](p)
+    wait_bytes(t.at[pl.ds(0, 15 * PAIRS)], t_send)
+    for p in range(PIECES):
+        wait_bytes(w_of(p).at[pl.ds(0, 7 * ROWS)], w_send.at[p])
     for p in range(EARLY, PIECES):
         whole(p)
-    for p in range(PIECES):
-        wait_bytes(w_of(p).at[pl.ds(0, 7 * ROWS)], w_send.at[p])
-    wait_bytes(t.at[pl.ds(0, 15 * PAIRS)], t_send)
-
-
-def finish_kernel(done, t, late, pe, vir_row, vir_in, out, tail, vir, vir_sem, sem):
-    col = lax.axis_index("col")
+
+
+def finish_kernel(done, t, late, pe, late_ve, out, tail, sem):
     width = EARLY * STRIP
     copies = [pltpu.make_async_copy(done, out.at[:, pl.ds(0, width)], sem.at[0])]
     copies[0].start()
-    vir_copy = pltpu.make_async_copy(vir_in, vir, vir_sem)
-    vir_copy.start()
-    vir_copy.wait()
     for k in range(PIECES - EARLY):
-        ve = vir[col * PIECES + EARLY + k] + vir_row[...]
-        ladder_tile(t, late.at[k], pe, ve, tail.at[k])
+        ladder_tile(t, late.at[k], pe, late_ve[:, k * STRIP : (k + 1) * STRIP], tail.at[k])
         copy = pltpu.make_async_copy(
             tail.at[k], out.at[:, pl.ds(width + k * STRIP, STRIP)], sem.at[k + 1]
         )
@@ -246,14 +243,14 @@
     vmem, hbm = pl.BlockSpec(memory_space=pltpu.VMEM), pl.BlockSpec(memory_space=pltpu.HBM)
     rows, depth, columns = 16 * PAIRS, 8 * ROWS, PIECES * STRIP
     late_count = PIECES - EARLY
-    done, t, late, pe, vir_row = pl.pallas_call(
+    done, t, late, pe, late_ve = pl.pallas_call(
         gather_kernel,
         out_shape=(
             pltpu.VMEM((rows, EARLY * STRIP), jnp.bfloat16),
             pltpu.VMEM((rows, depth), jnp.bfloat16),
             pltpu.VMEM((late_count, depth, STRIP), jnp.bfloat16),
             pltpu.VMEM((rows, 128), jnp.float32),
-            pltpu.VMEM((1, vir_energy.shape[0]), jnp.float32),
+            pltpu.VMEM((1, late_count * STRIP), jnp.float32),
         ),
         in_specs=[hbm] * 7,
         out_specs=(vmem,) * 5,
@@ -261,6 +258,7 @@
             pltpu.VMEM((EARLY, depth, STRIP), jnp.bfloat16),
             pltpu.VMEM((PAIRS, depth), jnp.bfloat16),
             pltpu.VMEM((2, rows), jnp.int32),
+            pltpu.VMEM((1, vir_energy.shape[0]), jnp.float32),
             pltpu.SMEM((2,), jnp.int32),
             pltpu.SMEM((200,), jnp.float32),
             pltpu.SMEM((512,), jnp.float32),
@@ -284,12 +282,10 @@
     return pl.pallas_call(
         finish_kernel,
         out_shape=jax.ShapeDtypeStruct((rows, columns), jnp.bfloat16),
-        in_specs=[vmem] * 5 + [hbm],
+        in_specs=[vmem] * 5,
         out_specs=hbm,
         scratch_shapes=[
             pltpu.VMEM((late_count, rows, STRIP), jnp.bfloat16),
-            pltpu.SMEM((512,), jnp.float32),
-            pltpu.SemaphoreType.DMA,
             pltpu.SemaphoreType.DMA((late_count + 1,)),
         ],
         cost_estimate=pl.CostEstimate(
@@ -299,7 +295,7 @@
         ),
         compiler_params=pltpu.CompilerParams(vmem_limit_bytes=32 << 20),
         name="finish",
-    )(done, t, late, pe, vir_row, pltpu.with_memory_space_constraint(vir_energy, pltpu.HBM))
+    )(done, t, late, pe, late_ve)
 
 
 def solution(mesh):

time: 41.7 us -> 41.6 us (level)
  no operation moved by 1% of the time
where the time goes in v3:
time: 41.6 us; the launch traced here: 41.4 us
  Pallas kernels  41.4 us (100%)
    pallas_call x1, Pallas kernels, shards(): pl.pallas_call(gather_kernel, out_shape=(pltpu.VMEM((rows, EARLY * STRIP)...  35.3 us
    pallas_call x1, Pallas kernels, shards(): pl.pallas_call(finish_kernel, out_shape=jax.ShapeDtypeStruct((rows, colum...  6.08 us

profile of v3, /device:TPU:0, one launch (start us, length us, event | category | flops | bytes accessed | tf_op | source)
XLA Modules:
  0.0 41.4 jit_solution(13603554275294841626)
XLA Ops:
  0.0 35.3 %gather.1 = (bf16[2048,2560]{1,0:T(8,128)(2,1)S(1)}, bf16[2048,512]{1,0:T(8,128)(2,1)S(1)}, bf16[3,512,512]{2,1,0:T(8,128)(2,1)S(1)}, f32[2048,128]{1,0:T(8,128)S(1)}, f32[1,1536]{1,0:T(1,128)S(1)}) custom-call(bf16[64,4096]{1,0:T(8,128)(2,1)} %ints.1, bf16[128,512]{1,0:T(8,128)(2,1)} %amps.1, s32[2,2048]{1,0:T(2,128)} %pair_list.1, s32[2]{0:T(128)} %order_in.1, ...), custom_call_target="tpu_custom_call" | custom-call | flops 5368709120 | bytes 4194304 | tf_op jit(solution)/shard_map/gather/pallas_call | solution.py:246
  35.3 6.1 %finish.1 = bf16[2048,4096]{1,0:T(8,128)(2,1)} custom-call(bf16[2048,2560]{1,0:T(8,128)(2,1)S(1)} %get-tuple-element.10.done, bf16[2048,512]{1,0:T(8,128)(2,1)S(1)} %get-tuple-element.11.t, bf16[3,512,512]{2,1,0:T(8,128)(2,1)S(1)} %get-tuple-element.12.late, f32[2048,128]{1,0:T(8,128)S(1)} %get-tuple-element.13.pe, f32[1,1536]{1,0:T(1,128)S(1)} %get-tuple-element.14.late_ve), custom_call_target="tpu_custom_call" | custom-call | flops 3221225472 | bytes 16777216 | tf_op jit(solution)/shard_map/finish/pallas_call | solution.py:282

commit v4 on v3

--- a/solution.py
+++ b/solution.py
@@ -58,8 +58,6 @@
     for copy in small:
         copy.start()
 
-    pl.semaphore_wait(barrier, 7)
-
     def t_rows(dy, dz, dc=0):
         zl, core = (col // 2) % 2, col % 2
         zl = zl + dz * (1 - 2 * zl)
@@ -83,11 +81,10 @@
         at = ((x + dx) % 4) * 2 + zh + dz * (1 - 2 * zh)
         return w_of(p).at[pl.ds(pl.multiple_of(at * ROWS + lo, 32), size)]
 
-    def w_copy(p, dx, dz, sem, peer, lo=0, size=ROWS, own=False):
-        dst = w_rows(p, dx, dz, lo, size)
-        src = ints.at[:, pl.ds(p * STRIP, STRIP)] if own else dst
+    def w_copy(p, dx, dz, sem, peer, lo=0, size=ROWS):
+        block = w_rows(p, dx, dz, lo, size)
         return pltpu.make_async_remote_copy(
-            src_ref=src, dst_ref=dst, send_sem=w_send.at[p], recv_sem=w_recv.at[p, sem],
+            src_ref=block, dst_ref=block, send_sem=w_send.at[p], recv_sem=w_recv.at[p, sem],
             device_id=peer, device_id_type=MESH,
         )
 
@@ -96,17 +93,19 @@
 
     own_in = []
     for p in range(PIECES):
-        own_in.append(
-            pltpu.make_async_copy(ints.at[:, pl.ds(p * STRIP, STRIP)], w_rows(p, 0, 0), local_sem.at[p])
-        )
+        copy = pltpu.make_async_copy(ints.at[:, pl.ds(p * STRIP, STRIP)], w_rows(p, 0, 0), local_sem.at[p])
+        copy.start()
+        own_in.append(copy)
+    pl.semaphore_wait(barrier, 7)
+    for copy in own_in:
+        copy.wait()
 
     def ox(p):
-        w_copy(p, 0, 0, 0 if p in FAR else 1, xr, own=True).start()
-        w_copy(p, 0, 0, 1 if p in FAR else 3, xl, own=True).start()
+        w_copy(p, 0, 0, 0 if p in FAR else 1, xr).start()
+        w_copy(p, 0, 0, 1 if p in FAR else 3, xl).start()
 
     def oz(p):
-        w_copy(p, 0, 0, 3 if p in FAR else 0, zz, own=True).start()
-        own_in[p].start()
+        w_copy(p, 0, 0, 3 if p in FAR else 0, zz).start()
 
     def nc(p):
         w_wait(p, 0, 1, 0)
@@ -201,7 +200,6 @@
         pltpu.make_async_copy(ref, ref, sem).wait()
 
     def whole(p):
-        own_in[p].wait()
         wait_bytes(w_of(p).at[pl.ds(0, 4 * ROWS)], w_recv.at[p, 3])
 
     def mul(p):

time: 41.6 us -> 41.4 us (level)
  no operation moved by 1% of the time
where the time goes in v4:
time: 41.4 us; the launch traced here: 41.2 us
  Pallas kernels  41.2 us (100%)
    pallas_call x1, Pallas kernels, shards(): pl.pallas_call(gather_kernel, out_shape=(pltpu.VMEM((rows, EARLY * STRIP)...  35.1 us
    pallas_call x1, Pallas kernels, shards(): pl.pallas_call(finish_kernel, out_shape=jax.ShapeDtypeStruct((rows, colum...  6.08 us

profile of v4, /device:TPU:0, one launch (start us, length us, event | category | flops | bytes accessed | tf_op | source)
XLA Modules:
  0.0 41.2 jit_solution(9026161158699023076)
XLA Ops:
  0.0 35.1 %gather.1 = (bf16[2048,2560]{1,0:T(8,128)(2,1)S(1)}, bf16[2048,512]{1,0:T(8,128)(2,1)S(1)}, bf16[3,512,512]{2,1,0:T(8,128)(2,1)S(1)}, f32[2048,128]{1,0:T(8,128)S(1)}, f32[1,1536]{1,0:T(1,128)S(1)}) custom-call(bf16[64,4096]{1,0:T(8,128)(2,1)} %ints.1, bf16[128,512]{1,0:T(8,128)(2,1)} %amps.1, s32[2,2048]{1,0:T(2,128)} %pair_list.1, s32[2]{0:T(128)} %order_in.1, ...), custom_call_target="tpu_custom_call" | custom-call | flops 5368709120 | bytes 4194304 | tf_op jit(solution)/shard_map/gather/pallas_call | solution.py:244
  35.1 6.1 %finish.1 = bf16[2048,4096]{1,0:T(8,128)(2,1)} custom-call(bf16[2048,2560]{1,0:T(8,128)(2,1)S(1)} %get-tuple-element.10.done, bf16[2048,512]{1,0:T(8,128)(2,1)S(1)} %get-tuple-element.11.t, bf16[3,512,512]{2,1,0:T(8,128)(2,1)S(1)} %get-tuple-element.12.late, f32[2048,128]{1,0:T(8,128)S(1)} %get-tuple-element.13.pe, f32[1,1536]{1,0:T(1,128)S(1)} %get-tuple-element.14.late_ve), custom_call_target="tpu_custom_call" | custom-call | flops 3221225472 | bytes 16777216 | tf_op jit(solution)/shard_map/finish/pallas_call | solution.py:280
